TPU v7x, 256 devices: a whole 4x4x8 slice. The times are simulated.
256 devices in a mesh: sect: 4 (over y), grp: 8 (over x, core), tp: 8 (over z).
Axes of the slice: x: 4, y: 4, z: 8, core: 2. Of those that a mesh axis runs over, the one named last changes fastest.
Arguments:
- prefix_tokens: bfloat16 [128, 256, 8192], P(('sect', 'grp'), None, 'tp'), may hold values from -8 to 8
- prefix_lengths: int32 [32], replicated, may hold values from 1 to 256, 5120 in all
- assignment: int32 [32, 1], replicated, may hold values from 0 to 23; in each aligned block of 32 rows (0 to 31, 32 to 63, ...) at most 3 rows name the same one
- norm_gain: bfloat16 [8192], P('tp'), may hold values from 0.099609375 to 1.8984375
- kv_weight: bfloat16 [8192, 2048], P('tp'), as said below
- query_weight: bfloat16 [8192, 8192], P(('sect', 'grp'), 'tp'), as said below
- decode_tokens: bfloat16 [32, 3, 8, 2, 8192], P(('sect', 'grp'), None, None, None, 'tp'), may hold values from -8 to 8
Outputs:
- completion_states: bfloat16 [32, 3, 8, 2, 8192], P(('sect', 'grp'), None, None, None, 'tp')
Inputs may be any that keep to these rules, and one draw needn't show every extreme that they name: `assignment`: each decode group takes at most 3 prefixes, and some group takes exactly 3. `prefix_lengths`: the longest prefix has exactly 256 tokens. `query_weight`: entries are at most 4 / sqrt(8192) in magnitude. `kv_weight`: entries are at most 4 / sqrt(8192) in magnitude.
All inputs are finite; a program needn't handle non-finite values.
Results may differ from a plain program's by a relative error of at most 0.0066.
Values may be sent and summed in bfloat16 or wider, within the bound.
A program may use at most 128 MiB of HBM per device.

v0:
```python
import jax
import jax.numpy as jnp
from jax import lax
from jax.sharding import PartitionSpec as P

H = 64
KVH = 8
HD = 128


def from_root(value, axis, source):
    kept = jnp.where(lax.axis_index(axis) == source, value, 0).astype(value.dtype)
    return lax.psum(kept, axis)


def slot_select(assign, group, slots):
    owned = (assign == group).astype(jnp.int32)
    count = owned.shape[0]
    order = jnp.arange(count, dtype=jnp.int32)
    before = (order[None, :] < order[:, None]).astype(jnp.int32)
    rank = jnp.sum(before * owned[None, :], axis=1)
    place = jnp.arange(slots, dtype=jnp.int32)
    return ((owned[None, :] == 1) & (rank[None, :] == place[:, None])).astype(jnp.float32)


def attend(query, keyt, valt, own_k, own_v, slot_len):
    inv = 1.0 / query.shape[-1] ** 0.5
    pre = jnp.einsum("jcsagd,jadl->jcsagl", query, keyt, preferred_element_type=jnp.float32) * inv
    own = jnp.einsum("jcsagd,jctad->jcsagt", query, own_k, preferred_element_type=jnp.float32) * inv
    length = keyt.shape[-1]
    steps = own.shape[-1]
    pos = jnp.arange(length, dtype=jnp.float32)
    mask_pre = (pos[None, :] < slot_len[:, None])[:, None, None, None, None, :]
    tri = jnp.arange(steps)[:, None] >= jnp.arange(steps)[None, :]
    mask_own = tri[None, None, :, None, None, :]
    top = jnp.maximum(
        jnp.max(jnp.where(mask_pre, pre, -jnp.inf), axis=-1),
        jnp.max(jnp.where(mask_own, own, -jnp.inf), axis=-1),
    )[..., None]
    e_pre = jnp.where(mask_pre, jnp.exp(pre - top), 0.0)
    e_own = jnp.where(mask_own, jnp.exp(own - top), 0.0)
    total = jnp.sum(e_pre, axis=-1, keepdims=True) + jnp.sum(e_own, axis=-1, keepdims=True)
    w_pre = (e_pre / total).astype(jnp.bfloat16)
    w_own = (e_own / total).astype(jnp.bfloat16)
    out = jnp.einsum("jcsagl,jadl->jcsagd", w_pre, valt, preferred_element_type=jnp.float32)
    out = out + jnp.einsum("jcsagt,jctad->jcsagd", w_own, own_v, preferred_element_type=jnp.float32)
    return out.astype(jnp.bfloat16)


def local(
    prefix_tokens, prefix_lengths, assignment, norm_gain, kv_weight, query_weight, decode_tokens
):
    n_tp = lax.axis_size("tp")
    n_grp = lax.axis_size("grp")
    sect_index = lax.axis_index("sect")
    grp_index = lax.axis_index("grp")
    tp_index = lax.axis_index("tp")
    held, length, local_width = prefix_tokens.shape
    width = local_width * n_tp
    kv_cols = kv_weight.shape[1]
    kv_local = kv_cols // n_tp
    heads_local = kv_local // (2 * HD)
    per_group = H // KVH
    prefix_rows = prefix_tokens.reshape(held * length, local_width).astype(jnp.float32)
    squares = lax.psum(jnp.sum(prefix_rows * prefix_rows, axis=1), "tp")
    scale = lax.rsqrt(squares / width + 1e-05)
    normed = (prefix_rows * scale[:, None] * norm_gain.astype(jnp.float32)[None, :]).astype(
        jnp.bfloat16
    )
    columns = kv_weight
    prefix_kv = lax.psum_scatter(
        lax.dot_general(
            columns, normed, (((0,), (1,)), ((), ())), preferred_element_type=jnp.float32
        ),
        "tp",
        scatter_dimension=0,
        tiled=True,
    ).astype(jnp.bfloat16)
    prefix_kv = prefix_kv.reshape(kv_local, held, length)
    arrived = from_root(prefix_kv, "sect", 0)
    slots, comp, steps = (decode_tokens.shape[1], decode_tokens.shape[2], decode_tokens.shape[3])
    assign = assignment[:, 0]
    lengths = prefix_lengths.astype(jnp.float32)
    group_id = (sect_index - 1) * n_grp + grp_index
    select = slot_select(assign, group_id, slots)
    slot_len = jnp.dot(select, lengths, precision=lax.Precision.HIGHEST)
    picks = select.astype(jnp.bfloat16)
    cache = jnp.einsum(
        "jp,cpl->jcl",
        picks,
        lax.all_gather(arrived, "grp", axis=1, tiled=True),
        preferred_element_type=jnp.float32,
    ).astype(jnp.bfloat16)
    cache = cache.reshape(slots, heads_local, 2, HD, length)
    rows = slots * comp * steps
    dec_local = decode_tokens.reshape(rows, local_width)
    dec_full, gain_full = (
        lax.all_gather(dec_local, "tp", axis=1, tiled=True),
        lax.all_gather(norm_gain, "tp", axis=0, tiled=True),
    )
    dec_values = dec_full.astype(jnp.float32)
    dec_scale = lax.rsqrt(jnp.mean(dec_values * dec_values, axis=1, keepdims=True) + 1e-05)
    dec_norm = (dec_values * dec_scale * gain_full.astype(jnp.float32)[None, :]).astype(
        jnp.bfloat16
    )
    own_cols = lax.dynamic_slice_in_dim(dec_norm, tp_index * local_width, local_width, 1)
    kv_partial = jnp.dot(own_cols, kv_weight, preferred_element_type=jnp.float32)
    dec_kv = lax.psum_scatter(kv_partial, "tp", scatter_dimension=1, tiled=True).astype(
        jnp.bfloat16
    )
    dec_kv = dec_kv.reshape(slots, comp, steps, heads_local, 2, HD)
    q_cols = query_weight.shape[1]
    columns = dec_norm
    query = jnp.dot(
        columns,
        lax.all_gather(query_weight, ("sect", "grp"), axis=0, tiled=True),
        preferred_element_type=jnp.float32,
    )
    query = query.astype(jnp.bfloat16).reshape(slots, comp, steps, heads_local, per_group, HD)
    out = attend(
        query, cache[:, :, 0], cache[:, :, 1], dec_kv[..., 0, :], dec_kv[..., 1, :], slot_len
    )
    out = out.reshape(1, slots, comp, steps, q_cols)
    return jnp.where(sect_index > 0, out, jnp.zeros_like(out))


def solution(mesh):
    placed = (
        P(("sect", "grp"), None, "tp"),
        P(),
        P(),
        P("tp"),
        P("tp", None),
        P(("sect", "grp"), "tp"),
        P(("sect", "grp"), None, None, None, "tp"),
    )
    return jax.shard_map(
        local,
        mesh=mesh,
        in_specs=placed,
        out_specs=P(("sect", "grp"), None, None, None, "tp"),
        check_vma=False,
    )
```

profile of v0, /device:TPU:17, one launch (start us, length us, event | category | flops | bytes accessed | tf_op | source)
XLA Modules:
  0.0 361.8 jit_solution(6936285499516016394)
XLA Ops:
  6.5 0.0 reduce-scatter.3.cloned.1.call-start
  6.5 2.1 multiply_reduce_fusion
  8.6 16.5 %psum.14 = f32[1024]{0:T(1024)S(1)} all-reduce(f32[1024]{0:T(1024)S(1)} %bitcast.109), channel_id=1, replica_groups=mesh['sect'=4,'grp'=8,'tp'=8] {'tp'}, use_global_device_ids=true, to_apply=%region_2.0 | all-reduce | flops 1024 | bytes 8192 | tf_op jit(solution)/shard_map/psum | solution.py:65
  25.1 0.0 copy-start
  25.1 0.8 convert_element_type.77
  26.0 2.3 fusion.1
  28.3 0.0 copy-done
  28.3 6.6 %convolution_bitcast_fusion = f32[2048,1024]{0,1:T(8,128)} fusion(bf16[1024,1024]{1,0:T(8,128)(2,1)S(1)} %fusion.1, bf16[1024,2048]{1,0:T(8,128)(2,1)S(1)} %copy-done), kind=kOutput, calls=%fused_computation | convolution fusion | flops 4294967296 | bytes 14680064 | tf_op jit(solution)/shard_map/dot_general | solution.py:72
  34.9 0.0 copy-start.2
  34.9 0.0 copy-start.1
  34.9 0.0 reduce-scatter.3.cloned.1.call-update
  35.0 0.0 all-reduce.2.cloned.1.call-start
  35.0 0.6 copy-done.2
  35.6 15.4 %all_gather.14 = bf16[8192]{0:T(1024)(128)(2,1)S(1)} all-gather(bf16[1024]{0:T(1024)(128)(2,1)S(1)} %copy-done.2), channel_id=1, replica_groups=mesh['sect'=4,'grp'=8,'tp'=8] {'tp'}, dimensions={0}, use_global_device_ids=true | all-gather | bytes 18432 | tf_op jit(solution)/shard_map/all_gather | solution.py:99
  51.1 0.0 copy-done.1
  51.1 25.6 %all_gather.13 = bf16[48,8192]{1,0:T(8,128)(2,1)S(1)} all-gather(bf16[48,1024]{1,0:T(8,128)(2,1)S(1)} %reshape.165), channel_id=1, replica_groups=mesh['sect'=4,'grp'=8,'tp'=8] {'tp'}, dimensions={1}, use_global_device_ids=true | all-gather | bytes 884736 | tf_op jit(solution)/shard_map/all_gather | solution.py:98
  76.8 0.3 fusion.4
  77.0 62.0 %reduce-scatter.3.cloned.1.call-done = f32[256,1024]{0,1:T(8,128)} async-done(((f32[2048,1024]{0,1:T(8,128)}), f32[256,1024]{0,1:T(8,128)}) %reduce-scatter.3.cloned.1.call-update) | async-done | bytes 1048592 | tf_op jit(solution)/shard_map/reduce_scatter | solution.py:71
  139.0 1.3 convert_select_fusion
  140.3 1.0 copy.19
  141.3 0.0 copy-start.3
  141.3 0.0 copy-start.4
  141.3 0.0 all-reduce.2.cloned.1.call-update
  141.3 0.0 reduce-scatter.5.cloned.1.call-start
  141.4 0.2 fusion.6
  141.6 3.8 %fusion.22 = f32[48,2048]{1,0:T(8,128)} fusion(bf16[1024,2048]{1,0:T(8,128)(2,1)} %param.11, bf16[48,8192]{1,0:T(8,128)(2,1)S(1)} %fusion.6, s32[]{:T(128)S(6)} %select_n.56), kind=kOutput, calls=%fused_computation.37 | convolution fusion | flops 201326592 | bytes 4685828 | tf_op jit(solution)/shard_map/dot_general | solution.py:107
  145.4 0.0 reduce-scatter.5.cloned.1.call-update
  145.4 0.0 all-gather.3.cloned.1.call-start
  145.5 40.0 %all-reduce.2.cloned.1.call-done = bf16[256,4,256]{2,0,1:T(8,128)(2,1)} async-done(((bf16[256,4,256]{2,0,1:T(8,128)(2,1)}), bf16[256,4,256]{2,0,1:T(8,128)(2,1)}) %all-reduce.2.cloned.1.call-update) | async-done | bytes 524304 | tf_op jit(solution)/shard_map/psum | solution.py:13
  185.5 0.0 all-gather.3.cloned.1.call-update
  185.5 0.0 all-gather.5.cloned.1.call-start
  185.6 0.5 all-gather.5.cloned.1.call-update
  186.1 0.0 copy-done.3
  186.2 0.1 select_reduce_fusion.2
  186.3 0.0 copy-done.4
  186.3 0.1 convolution_bitcast_fusion.3
  186.4 0.1 iota_compare_fusion.1
  186.5 37.2 %reduce-scatter.5.cloned.1.call-done = f32[48,256]{1,0:T(8,128)} async-done(((f32[48,2048]{1,0:T(8,128)}), f32[48,256]{1,0:T(8,128)}) %reduce-scatter.5.cloned.1.call-update) | async-done | bytes 49168 | tf_op jit(solution)/shard_map/reduce_scatter | solution.py:108
  223.7 0.8 convert_element_type.86
  224.5 39.5 %all-gather.3.cloned.1.call-done = bf16[256,32,256]{2,0,1:T(8,128)(2,1)} async-done(((bf16[256,4,256]{2,0,1:T(8,128)(2,1)}), bf16[256,32,256]{2,0,1:T(8,128)(2,1)}) %all-gather.3.cloned.1.call-update) | async-done | bytes 4194320 | tf_op jit(solution)/shard_map/all_gather | solution.py:91
  264.0 4.6 %fusion.7 = bf16[3,256,256]{2,0,1:T(4,128)(2,1)S(1)} fusion(bf16[256,32,256]{2,0,1:T(8,128)(2,1)} %all-gather.3.cloned.1.call-done, s32[32]{0:T(128)S(1)} %select_reduce_fusion.2, pred[32]{0:T(512)(128)(4,1)S(1)} %get-tuple-element.5), kind=kOutput, calls=%fused_computation.12 | convolution fusion | flops 12779904 | bytes 4587680 | tf_op jit(solution)/shard_map/jp,cpl->jcl/dot_general | solution.py:88
  268.6 0.2 fusion.39
  268.8 75.0 %all-gather.5.cloned.1.call-done = bf16[8192,1024]{1,0:T(8,128)(2,1)} async-done(((bf16[256,1024]{1,0:T(8,128)(2,1)}), bf16[8192,1024]{1,0:T(8,128)(2,1)}) %all-gather.5.cloned.1.call-update) | async-done | bytes 16777232 | tf_op jit(solution)/shard_map/all_gather | solution.py:116
  343.9 8.8 %fusion.13 = bf16[6,8,8,128]{3,1,2,0:T(8,128)(2,1)S(1)} fusion(bf16[48,8192]{1,0:T(8,128)(2,1)S(1)} %fusion.6, bf16[8192,1024]{1,0:T(8,128)(2,1)} %all-gather.5.cloned.1.call-done), kind=kOutput, calls=%fused_computation.20 | convolution fusion | flops 805355520 | bytes 17661952 | tf_op jit(solution)/shard_map/dot_general | solution.py:114
  352.7 0.6 select_reduce_fusion.1
  353.3 0.3 select_reduce_fusion
  353.6 0.2 fusion.26
  353.7 0.3 bitcast_reduce_fusion
  354.0 0.3 convolution_bitcast_fusion.1
  354.3 0.3 fusion.14
  354.6 0.7 select_n.62
  (12 shorter events, 0.2 us)
Async XLA Ops:
  6.5 132.5 %reduce-scatter.3.cloned.1.call-start = ((), (), s32[]{:S(2)}) async-start(), calls=%async_computation.2 | async-start | bytes 9437184 | tf_op jit(solution)/shard_map/reduce_scatter | solution.py:71
  25.1 3.2 copy-start
  34.9 0.7 copy-start.2
  34.9 16.1 %copy-start.1 = (bf16[1,3,8,2,1024]{4,3,2,1,0:T(2,128)(2,1)S(1)}, bf16[1,3,8,2,1024]{4,3,2,1,0:T(2,128)(2,1)}, u32[]{:S(2)}) copy-start(bf16[1,3,8,2,1024]{4,3,2,1,0:T(2,128)(2,1)} %param.13) | copy-start | bytes 294916
  35.0 150.5 %all-reduce.2.cloned.1.call-start = ((), (), s32[]{:S(2)}) async-start(), calls=%async_computation.3 | async-start | bytes 1048576 | tf_op jit(solution)/shard_map/psum | solution.py:13
  141.3 44.9 %copy-start.3 = (s32[32,1]{0,1:T(1,128)S(1)}, s32[32,1]{0,1:T(1,128)}, u32[]{:S(2)}) copy-start(s32[32,1]{0,1:T(1,128)} %param.9) | copy-start | bytes 388
  141.3 45.0 %copy-start.4 = (s32[32]{0:T(128)S(1)}, s32[32]{0:T(128)}, u32[]{:S(2)}) copy-start(s32[32]{0:T(128)} %param.8) | copy-start | bytes 388
  141.3 82.4 %reduce-scatter.5.cloned.1.call-start = ((), (), s32[]{:S(2)}) async-start(), calls=%async_computation.6 | async-start | bytes 442368 | tf_op jit(solution)/shard_map/reduce_scatter | solution.py:108
  145.4 118.6 %all-gather.3.cloned.1.call-start = ((), (), s32[]{:S(2)}) async-start(), calls=%async_computation.4 | async-start | bytes 4718592 | tf_op jit(solution)/shard_map/all_gather | solution.py:91
  185.5 158.3 %all-gather.5.cloned.1.call-start = ((), (), s32[]{:S(2)}) async-start(), calls=%async_computation.5 | async-start | bytes 17301504 | tf_op jit(solution)/shard_map/all_gather | solution.py:116
Sparse Core Ops, SparseCore 0:
  35.1 103.8 reduce-scatter.2
  141.4 44.0 all-reduce.1
  188.0 35.6 reduce-scatter.4
  225.5 38.4 all-gather.2
  266.7 77.0 all-gather.4
where the time goes:
time: 364 us; the launch traced here: 362 us
  waiting for transfers between devices  254 us (70%)
  blocking collectives  57.6 us (16%)
  matrix products  25.4 us (7%)
  between operations  13.3 us (4%)
  other arithmetic  8.49 us (2%)
    all_gather x1, waiting for transfers between devices, local(): lax.all_gather(query_weight, ('sect', 'grp'), axis=0, tiled=True)  75 us
    reduce_scatter x1, waiting for transfers between devices, local(): lax.psum_scatter(lax.dot_general(columns, normed, (((0,), (1,)), ((), ())...  62 us
    psum x1, waiting for transfers between devices, from_root(): return lax.psum(kept, axis)  40 us
    all_gather x1, waiting for transfers between devices, local(): lax.all_gather(arrived, 'grp', axis=1, tiled=True)  39.5 us
    reduce_scatter x1, waiting for transfers between devices, local(): lax.psum_scatter(kv_partial, 'tp', scatter_dimension=1, tiled=True)  37.2 us
    all_gather x1, blocking collectives, local(): lax.all_gather(dec_local, 'tp', axis=1, tiled=True)  25.6 us
    psum x1, blocking collectives, local(): squares = lax.psum(jnp.sum(prefix_rows * prefix_rows, axis=1), 'tp')  16.5 us
    all_gather x1, blocking collectives, local(): lax.all_gather(norm_gain, 'tp', axis=0, tiled=True)  15.4 us
  transfers between devices with their start and end apart: 5, of which 5 were waited for; matrix products, arithmetic and copies ran while one was open for 3% of the time, Pallas kernels for 0%

commit v1 on v0

v1 whole, which is shorter than its diff:
```python
import functools

import jax
import jax.numpy as jnp
from jax import lax
from jax.experimental import pallas as pl
from jax.experimental.pallas import tpu as pltpu
from jax.sharding import PartitionSpec as P

MESH = pl.DeviceIdType.MESH
F32 = jnp.float32
BF16 = jnp.bfloat16
H, KVH, HD = 64, 8, 128
NT = 8
ROWS = 48
EPS = 1e-05


def kernel(
    assign,
    lens,
    gain,
    dec,
    tok,
    wkv,
    wq,
    out,
    wkv_v,
    tokv,
    xp,
    xag,
    xin,
    wq_v,
    ssp,
    ssd,
    dks,
    dkr,
    qs,
    qr,
    send_l,
    recv_l,
    send_s,
    recv_s,
    kv,
    lsem,
    ssem,
    rsem,
):
    s, g, t = lax.axis_index("sect"), lax.axis_index("grp"), lax.axis_index("tp")
    core = lax.rem(g, 2)
    sib = g + 1 - 2 * core
    xr, xl = lax.rem(g + 2, 8), lax.rem(g + 6, 8)
    xo = lax.rem(g + 4, 8)

    def zed(k):
        return lax.rem(t + (k + 2 * NT), NT)

    def sec(k):
        return lax.rem(s + k, 4)

    counts = {"s": 0, "r": 0}

    def new(kind, number=1):
        first = counts[kind]
        counts[kind] += number
        return first

    pending = []

    def remote(src, dst, snd, rcv, dev):
        return pltpu.make_async_remote_copy(
            src_ref=src,
            dst_ref=dst,
            send_sem=ssem.at[snd],
            recv_sem=rsem.at[rcv],
            device_id=dev,
            device_id_type=MESH,
        )

    def push(src, dst, rcv, dev, like, guard=None):
        snd = new("s")
        remote(src, dst, snd, rcv, dev).start()
        pending.append((guard, like, snd))

    def arrive(dst, rcv):
        remote(dst, dst, 0, rcv, (s, sib, t)).wait_recv()

    def when(cond):
        return pl.when(cond)

    decoding = s > 0
    root = s == 0
    first, third = s == 1, s == 3
    side = first | third

    load_wkv = pltpu.make_async_copy(wkv, wkv_v, lsem.at[0])
    load_wkv.start()
    load_wq = pltpu.make_async_copy(wq, wq_v.at[pl.ds(g * 256, 256)], lsem.at[1])
    load_wq.start()

    def load_tok(i):
        return pltpu.make_async_copy(tok.at[2 * i], tokv.at[i], lsem.at[2 + i])

    @when(root)
    def _():
        load_tok(0).start()
        load_tok(1).start()

    barrier = pltpu.get_barrier_semaphore()
    friends = [(s, g, zed(k)) for k in range(1, NT)]
    friends += [(sec(k), g, t) for k in (1, 2, 3)]
    friends += [(s, xr, t), (s, xl, t), (s, sib, t)]
    for dev in friends:
        pl.semaphore_signal(barrier, inc=1, device_id=dev, device_id_type=MESH)
    pl.semaphore_wait(barrier, len(friends))

    r_tok = new("r", 2)
    HB = 128

    def tok_half():
        return tokv.at[0, 0:HB]

    def w_block():
        return wq_v.at[0:256]

    def w_half():
        return wq_v.at[0:128]

    def kv_half():
        return kv.at[0, 0:128]

    @when(root)
    def _():
        for u in range(2):
            rows = pl.ds(u * HB, HB)
            push(tok.at[1, rows], tokv.at[0, rows], r_tok + u, (1, g, t), tok_half, root)
            push(tok.at[3, rows], tokv.at[0, rows], r_tok + u, (3, g, t), tok_half, root)

    r_w = new("r", 5)
    r_ws = new("r", 4)
    mine = pl.ds(g * 256, 256)
    push(wq, wq_v.at[mine], r_w, (s, xr, t), w_block)
    push(wq, wq_v.at[mine], r_w + 1, (s, xl, t), w_block)
    push(wq, wq_v.at[mine], r_ws, (s, sib, t), w_block)

    gain_f = gain[...].astype(F32)
    ones = jnp.ones((8, 1024), BF16)
    nt_dims = (((1,), (1,)), ((), ()))

    r_xag = new("r", 8)
    r_ssd = new("r", 8)
    r_dkv = new("r", 8)
    r_xin = new("r", 6)

    def to_section(shift):
        q = zed(shift)
        dest = q // 2
        snd = new("s")
        rcv = r_xin + (s - 1) * 2 + lax.rem(q, 2)
        src = xag.at[q]
        dst = xin.at[lax.rem(q, 2), pl.ds((s - 1) * ROWS, ROWS)]

        @when(dest != s)
        def _():
            remote(src, dst, snd, rcv, (dest, g, t)).start()

        pending.append((lambda: decoding & (zed(shift) // 2 != s), lambda: xag.at[0], snd))

    @when(decoding)
    def _():
        x = dec[...].astype(F32)
        xag[t] = (x * gain_f).astype(BF16)
        push(xag.at[t], xag.at[t], r_xag, (s, g, zed(1)), lambda: xag.at[0], decoding)
        push(xag.at[t], xag.at[t], r_xag + 4, (s, g, zed(-1)), lambda: xag.at[0], decoding)
        to_section(0)
        square = lax.dot_general(
            ones, (x * x).astype(BF16), nt_dims, preferred_element_type=F32
        )
        ssd[t] = jnp.concatenate([square, jnp.zeros((8, 128 - ROWS), F32)], axis=1)
        for k in range(1, NT):
            push(ssd.at[t], ssd.at[t], r_ssd + k, (s, g, zed(k)), lambda: ssd.at[0], decoding)

    load_wkv.wait()

    @when(decoding)
    def _():
        for a in range(NT):
            dks[a] = jnp.dot(
                xag[t], wkv_v[:, a * 256 : (a + 1) * 256], preferred_element_type=F32
            ).astype(BF16)
        for k in range(1, NT):
            a = zed(k)
            push(dks.at[a], dkr.at[t], r_dkv + k, (s, g, a), lambda: dks.at[0], decoding)
        for k in range(1, 5):
            low, high = zed(-k), zed(k)
            arrive(xag.at[low], r_xag + k - 1)
            if k < 4:
                push(xag.at[low], xag.at[low], r_xag + k, (s, g, zed(1)), lambda: xag.at[0], decoding)
                arrive(xag.at[high], r_xag + 4 + k - 1)
                if k < 3:
                    push(xag.at[high], xag.at[high], r_xag + 4 + k, (s, g, zed(-1)), lambda: xag.at[0], decoding)
                to_section(k)
            to_section(-k)

    def forward_w():
        left, right = pl.ds(xl * 256, 128), pl.ds(xr * 256 + 128, 128)
        arrive(wq_v.at[pl.ds(xl * 256, 256)], r_w)
        push(wq_v.at[left], wq_v.at[left], r_w + 2, (s, xr, t), w_half)
        arrive(wq_v.at[pl.ds(xr * 256, 256)], r_w + 1)
        push(wq_v.at[right], wq_v.at[right], r_w + 3, (s, xl, t), w_half)
        whole = pl.ds(xl * 256, 256)
        push(wq_v.at[whole], wq_v.at[whole], r_ws + 1, (s, sib, t), w_block)
        whole = pl.ds(xr * 256, 256)
        push(wq_v.at[whole], wq_v.at[whole], r_ws + 2, (s, sib, t), w_block)

    def finish_w():
        load_wq.wait()
        arrive(wq_v.at[pl.ds(xo * 256, 128)], r_w + 2)
        arrive(wq_v.at[pl.ds(xo * 256 + 128, 128)], r_w + 3)
        whole = pl.ds(xo * 256, 256)
        push(wq_v.at[whole], wq_v.at[whole], r_ws + 3, (s, sib, t), w_block)
        for n, other in enumerate((g, xl, xr, xo)):
            block = other + 1 - 2 * core
            arrive(wq_v.at[pl.ds(block * 256, 256)], r_ws + n)

    r_long = new("r", 8)
    r_short = new("r", 6)
    r_ssp = new("r", 16)

    def part(i, head):
        return jnp.dot(
            xp[i],
            wkv_v[:, pl.ds(pl.multiple_of(head * 256, 256), 256)],
            preferred_element_type=F32,
        )

    def prepare(i, guard):
        rows = tokv[i].astype(F32)
        xp[i] = (rows * gain_f).astype(BF16)
        ssp[i, t] = lax.dot_general(
            ones, (rows * rows).astype(BF16), nt_dims, preferred_element_type=F32
        )
        for k in range(1, NT):
            push(ssp.at[i, t], ssp.at[i, t], r_ssp + 8 * i + k, (s, g, zed(k)), lambda: ssp.at[0, 0], guard)

    def ring(i, k, guard):
        way = -1 if i == 0 else 1
        if k < 4:
            value = part(i, zed(way * (4 - k)))
            if k > 0:
                arrive(recv_l.at[i, k - 1], r_long + 4 * i + k - 1)
                value = value + recv_l[i, k - 1].astype(F32)
            send_l[i, k] = value.astype(BF16)
            push(send_l.at[i, k], recv_l.at[i, k], r_long + 4 * i + k, (s, g, zed(way)), lambda: send_l.at[0, 0], guard)
        if k < 3:
            value = part(i, zed(-way * (3 - k)))
            if k > 0:
                arrive(recv_s.at[i, k - 1], r_short + 3 * i + k - 1)
                value = value + recv_s[i, k - 1].astype(F32)
            send_s[i, k] = value.astype(BF16)
            push(send_s.at[i, k], recv_s.at[i, k], r_short + 3 * i + k, (s, g, zed(-way)), lambda: send_l.at[0, 0], guard)

    def column(row):
        return jnp.broadcast_to(row, (128, 128)).T

    def settle(i, slot):
        value = part(i, t)
        total = jnp.zeros((8, 256), F32)
        for k in range(1, NT):
            arrive(ssp.at[i, zed(-k)], r_ssp + 8 * i + k)
        for n in range(NT):
            total = total + ssp[i, n]
        scale = lax.rsqrt(total[0:1] / (NT * 1024) + EPS)
        arrive(recv_l.at[i, 3], r_long + 4 * i + 3)
        arrive(recv_s.at[i, 2], r_short + 3 * i + 2)
        value = value + recv_l[i, 3].astype(F32) + recv_s[i, 2].astype(F32)
        for u in range(2):
            by = column(scale[:, u * 128 : (u + 1) * 128])
            half = value[u * 128 : (u + 1) * 128]
            kv[slot, u * 128 : (u + 1) * 128] = jnp.concatenate(
                [half[:, :128] * by, half[:, 128:] * by], axis=1
            ).astype(BF16)

    r_y = new("r", 4)
    here = [4 * g + j for j in range(4)]

    def send_y(j, sections, guard):
        for dest in sections:
            push(kv.at[here[j]], kv.at[here[j]], r_y + j, (dest, g, t), lambda: kv.at[0], guard)

    r_q = new("r", 4)

    def queries():
        finish_w()

        @when(decoding)
        def _():
            for b in range(2):
                xin[b, pl.ds((s - 1) * ROWS, ROWS)] = xag[2 * s + b]

        for other in (1, 2, 3):

            @when(s != other)
            def _():
                for b in range(2):
                    arrive(
                        xin.at[b, (other - 1) * ROWS : other * ROWS], r_xin + (other - 1) * 2 + b
                    )

        for n in range(4):
            cols = slice(n * 256, (n + 1) * 256)
            value = jnp.dot(xin[0], wq_v[0:1024, cols], preferred_element_type=F32)
            value = value + jnp.dot(xin[1], wq_v[1024:2048, cols], preferred_element_type=F32)
            for dest in range(3):
                qs[dest, :, cols] = value[dest * ROWS : (dest + 1) * ROWS].astype(BF16)
        for dest in (1, 2, 3):
            snd = new("s")

            @when(s != dest)
            def _():
                remote(qs.at[dest - 1], qr.at[s], snd, r_q + s, (dest, g, t)).start()

            pending.append((s != dest, lambda: qs.at[0], snd))

    @when(root)
    def _():
        load_tok(0).wait()
        prepare(0, root)
        ring(0, 0, root)
        ring(0, 1, root)
        load_tok(1).wait()
        prepare(1, root)

    @when(side)
    def _():
        for u in range(2):
            arrive(tokv.at[0, u * HB : (u + 1) * HB], r_tok + u)
        prepare(0, side)
        ring(0, 0, side)
        ring(0, 1, side)

    forward_w()

    @when(root)
    def _():
        ring(0, 2, root)
        ring(1, 0, root)
        ring(0, 3, root)
        ring(1, 1, root)
        settle(0, here[0])
        send_y(0, (1, 3), root)
        ring(1, 2, root)

    @when(side)
    def _():
        ring(0, 2, side)
        ring(0, 3, side)

        @when(s == 1)
        def _():
            settle(0, here[1])
            send_y(1, (2, 3), first)

        @when(s == 3)
        def _():
            settle(0, here[3])
            send_y(3, (2, 1), third)

    queries()

    @when(root)
    def _():
        ring(1, 3, root)
        settle(1, here[2])
        send_y(2, (1, 3), root)

    r_x = new("r", 16)
    r_c = new("r", 16)

    def entry(j):
        if j == 0:

            @when(decoding)
            def _():
                arrive(kv.at[here[0]], r_y)

            @when(s == 1)
            def _():
                send_y(0, (2,), first)
        elif j == 2:

            @when(decoding)
            def _():
                arrive(kv.at[here[2]], r_y + 2)

            @when(s == 3)
            def _():
                send_y(2, (2,), third)
        else:

            @when(decoding & (s != j))
            def _():
                arrive(kv.at[here[j]], r_y + j)

        @when(decoding)
        def _():
            block = kv.at[here[j]]
            push(block, block, r_x + 4 * j, (s, xr, t), lambda: kv.at[0], decoding)
            push(block, block, r_x + 4 * j + 1, (s, xl, t), lambda: kv.at[0], decoding)
            push(block, block, r_c + 4 * j, (s, sib, t), lambda: kv.at[0], decoding)

    def relay(j):
        left, right = 4 * xl + j, 4 * xr + j
        arrive(kv.at[left], r_x + 4 * j)
        part_l = kv.at[left, 0:128]
        push(part_l, part_l, r_x + 4 * j + 2, (s, xr, t), kv_half, decoding)
        arrive(kv.at[right], r_x + 4 * j + 1)
        part_r = kv.at[right, 128:256]
        push(part_r, part_r, r_x + 4 * j + 3, (s, xl, t), kv_half, decoding)
        push(kv.at[left], kv.at[left], r_c + 4 * j + 1, (s, sib, t), lambda: kv.at[0], decoding)
        push(kv.at[right], kv.at[right], r_c + 4 * j + 2, (s, sib, t), lambda: kv.at[0], decoding)

    def opposite(j):
        block = 4 * xo + j
        arrive(kv.at[block, 0:128], r_x + 4 * j + 2)
        arrive(kv.at[block, 128:256], r_x + 4 * j + 3)
        push(kv.at[block], kv.at[block], r_c + 4 * j + 3, (s, sib, t), lambda: kv.at[0], decoding)

    def crossed(j):
        for n, other in enumerate((g, xl, xr, xo)):
            arrive(kv.at[4 * (other + 1 - 2 * core) + j], r_c + 4 * j + n)

    for j in (0, 1, 3):
        entry(j)

    @when(decoding)
    def _():
        relay(0)

    entry(2)

    @when(decoding)
    def _():
        relay(1)
        relay(3)
        opposite(0)
        relay(2)
        opposite(1)
        opposite(3)
        opposite(2)

    inv = 1.0 / HD**0.5

    @when(root)
    def _():
        out[...] = jnp.zeros(out.shape, out.dtype)

    @when(decoding)
    def _():
        for k in range(1, NT):
            arrive(ssd.at[zed(-k)], r_ssd + k)
            arrive(dkr.at[zed(-k)], r_dkv + k)
        total = jnp.zeros((8, 128), F32)
        for n in range(NT):
            total = total + ssd[n]
        scale = column(lax.rsqrt(total[0:1] / (NT * 1024) + EPS))[:ROWS]
        dkr[t] = dks[t]
        own = jnp.zeros((ROWS, 256), F32)
        for n in range(NT):
            own = own + dkr[n].astype(F32)
        own_k = (own[:, :128] * scale).astype(BF16)
        own_v = (own[:, 128:] * scale).astype(BF16)
        for src in range(4):

            @when(s != src)
            def _():
                arrive(qr.at[src], r_q + src)

            if src > 0:

                @when(s == src)
                def _():
                    qr[src] = qs[src - 1]

        for j in range(4):
            crossed(j)
        group = (s - 1) * 8 + g

        def pick(p, carry):
            seen, i0, i1, i2, n0, n1, n2 = carry
            hit = (assign[p] == group).astype(jnp.int32)
            length = lens[p]
            h0 = hit * (seen == 0).astype(jnp.int32)
            h1 = hit * (seen == 1).astype(jnp.int32)
            h2 = hit * (seen == 2).astype(jnp.int32)
            return (
                seen + hit,
                i0 + h0 * p,
                i1 + h1 * p,
                i2 + h2 * p,
                n0 + h0 * length,
                n1 + h1 * length,
                n2 + h2 * length,
            )

        zero = jnp.int32(0)
        picked = lax.fori_loop(0, assign.shape[0], pick, (zero,) * 7)
        low = jnp.float32(-1e30)
        pos = lax.broadcasted_iota(jnp.int32, (128, 256), 1)
        row = lax.rem(lax.broadcasted_iota(jnp.int32, (128, 16), 0), 16)
        col = lax.broadcasted_iota(jnp.int32, (128, 16), 1)
        mask_own = (row // 2 == col // 2) & (col <= row)
        for j in range(3):
            rows = slice(j * 16, (j + 1) * 16)
            block = kv[picked[1 + j]]
            keys, values = block[:, :128], block[:, 128:]
            raw = jnp.zeros((16, 1024), F32)
            for src in range(4):
                raw = raw + qr[src, rows].astype(F32)
            by = scale[rows]
            q = jnp.concatenate(
                [raw[:, h * 128 : (h + 1) * 128] * by for h in range(8)], axis=0
            ).astype(BF16)
            pre = lax.dot_general(q, keys, nt_dims, preferred_element_type=F32) * inv
            self_ = lax.dot_general(q, own_k[rows], nt_dims, preferred_element_type=F32) * inv
            mask_pre = pos < picked[4 + j]
            pre = jnp.where(mask_pre, pre, low)
            self_ = jnp.where(mask_own, self_, low)
            top = jnp.maximum(
                jnp.max(pre, axis=1, keepdims=True), jnp.max(self_, axis=1, keepdims=True)
            )
            e_pre = jnp.where(mask_pre, jnp.exp(pre - top), 0.0)
            e_own = jnp.where(mask_own, jnp.exp(self_ - top), 0.0)
            norm = jnp.sum(e_pre, axis=1, keepdims=True) + jnp.sum(e_own, axis=1, keepdims=True)
            w_pre = (e_pre / norm).astype(BF16)
            w_own = (e_own / norm).astype(BF16)
            o = jnp.dot(w_pre, values, preferred_element_type=F32)
            o = o + jnp.dot(w_own, own_v[rows], preferred_element_type=F32)
            o = o.astype(BF16)
            for h in range(8):
                out[rows, h * 128 : (h + 1) * 128] = o[h * 16 : (h + 1) * 16]

    for guard, like, snd in pending:

        def done(like=like, snd=snd):
            remote(like(), like(), snd, 0, (s, sib, t)).wait_send()

        if guard is None:
            done()
        else:
            when(guard() if callable(guard) else guard)(done)

    assert counts["s"] <= N_SEND and counts["r"] <= N_RECV, counts


N_SEND = 200
N_RECV = 140


def local(
    prefix_tokens, prefix_lengths, assignment, norm_gain, kv_weight, query_weight, decode_tokens
):
    shape = decode_tokens.shape
    dec = decode_tokens.reshape(ROWS, 1024)
    smem = pl.BlockSpec(memory_space=pltpu.SMEM)
    vmem = pl.BlockSpec(memory_space=pltpu.VMEM)
    anywhere = pl.BlockSpec(memory_space=pl.ANY)
    result = pl.pallas_call(
        kernel,
        out_shape=jax.ShapeDtypeStruct((ROWS, 1024), BF16),
        in_specs=[smem, smem, vmem, vmem, anywhere, anywhere, anywhere],
        out_specs=vmem,
        scratch_shapes=[
            pltpu.VMEM((1024, 2048), BF16),
            pltpu.VMEM((2, 256, 1024), BF16),
            pltpu.VMEM((2, 256, 1024), BF16),
            pltpu.VMEM((8, ROWS, 1024), BF16),
            pltpu.VMEM((2, 3 * ROWS, 1024), BF16),
            pltpu.VMEM((2048, 1024), BF16),
            pltpu.VMEM((2, 8, 8, 256), F32),
            pltpu.VMEM((8, 8, 128), F32),
            pltpu.VMEM((8, ROWS, 256), BF16),
            pltpu.VMEM((8, ROWS, 256), BF16),
            pltpu.VMEM((3, ROWS, 1024), BF16),
            pltpu.VMEM((4, ROWS, 1024), BF16),
            pltpu.VMEM((2, 4, 256, 256), BF16),
            pltpu.VMEM((2, 4, 256, 256), BF16),
            pltpu.VMEM((2, 3, 256, 256), BF16),
            pltpu.VMEM((2, 3, 256, 256), BF16),
            pltpu.VMEM((32, 256, 256), BF16),
            pltpu.SemaphoreType.DMA((4,)),
            pltpu.SemaphoreType.DMA((N_SEND,)),
            pltpu.SemaphoreType.DMA((N_RECV,)),
        ],
        compiler_params=pltpu.CompilerParams(
            collective_id=0, has_side_effects=True, vmem_limit_bytes=40 * 2**20
        ),
    )(
        assignment[:, 0],
        prefix_lengths,
        norm_gain.reshape(1, 1024),
        dec,
        prefix_tokens,
        kv_weight,
        query_weight,
    )
    return result.reshape(shape)


def solution(mesh):
    placed = (
        P(("sect", "grp"), None, "tp"),
        P(),
        P(),
        P("tp"),
        P("tp", None),
        P(("sect", "grp"), "tp"),
        P(("sect", "grp"), None, None, None, "tp"),
    )
    return jax.shard_map(
        local,
        mesh=mesh,
        in_specs=placed,
        out_specs=P(("sect", "grp"), None, None, None, "tp"),
        check_vma=False,
    )
```

time: 364 us -> 92 us (0.25)
  waiting for transfers between devices: 254 us -> 0 us
  Pallas kernels: 0 us -> 83.3 us
  blocking collectives: 57.6 us -> 0 us
  matrix products: 25.4 us -> 0 us
  between operations: 13.3 us -> 0.02 us
  other arithmetic: 8.49 us -> 0 us
  local copies, waits for them, and re-layouts: 2.58 us -> 8.42 us
    all_gather x2 -> x0, waiting for transfers between devices: 115 us -> none  [the longest x1 75 us: local(): lax.all_gather(query_weight, ('sect', 'grp'), axis=0, tiled=True)]
    reduce_scatter x2 -> x0, waiting for transfers between devices: 99.2 us -> none  [the longest x1 62 us: local(): lax.psum_scatter(lax.dot_general(columns, normed, (((0,), (1,)), ((), ())...]
    pallas_call x0 -> x1, Pallas kernels: none -> 83.3 us  [local(): pl.pallas_call(kernel, out_shape=jax.ShapeDtypeStruct((ROWS, 1024), BF16)...]
    all_gather x2 -> x0, blocking collectives: 41.1 us -> none  [the longest x1 25.6 us: local(): lax.all_gather(dec_local, 'tp', axis=1, tiled=True)]
    psum x1 -> x0, waiting for transfers between devices: 40 us -> none  [from_root(): return lax.psum(kept, axis)]
    dot_general x9 -> x0, matrix products: 25.4 us -> none  [the longest x1 8.79 us: local(): jnp.dot(columns, lax.all_gather(query_weight, ('sect', 'grp'), axis=0, ti...]
    psum x1 -> x0, blocking collectives: 16.5 us -> none  [local(): squares = lax.psum(jnp.sum(prefix_rows * prefix_rows, axis=1), 'tp')]
    unnamed x12 -> x10, local copies, waits for them, and re-layouts: 0.64 us -> 6.12 us
  transfers between devices with their start and end apart: 5 -> 0, of which waited for: 5 -> 0; matrix products, arithmetic and copies ran while one was open for 3% -> 0% of each run, Pallas kernels for 0% -> 0%
where the time goes in v1:
time: 92 us; the launch traced here: 91.8 us
  Pallas kernels  83.3 us (91%)
  local copies, waits for them, and re-layouts  8.42 us (9%)
    pallas_call x1, Pallas kernels, local(): pl.pallas_call(kernel, out_shape=jax.ShapeDtypeStruct((ROWS, 1024), BF16)...  83.3 us
    unnamed x10, local copies, waits for them, and re-layouts  6.12 us

profile of v1, /device:TPU:17, one launch (start us, length us, event | category | flops | bytes accessed | tf_op | source)
XLA Modules:
  0.0 91.8 jit_solution(12198001194007853071)
XLA Ops:
  0.0 0.7 reshape.9.gain
  0.7 0.9 %reshape.10.dec = bf16[48,1024]{1,0:T(8,128)(2,1)S(1)} reshape(bf16[1,3,8,2,1024]{4,3,2,1,0:T(2,128)(2,1)} %param.13) | data formatting | bytes 196608 | tf_op jit(solution)/shard_map/reshape | solution.py:564
  1.6 0.0 copy-start
  1.6 2.2 %copy-done = bf16[1024,2048]{1,0:T(8,128)(2,1)S(1)} copy-done((bf16[1024,2048]{1,0:T(8,128)(2,1)S(1)}, bf16[1024,2048]{1,0:T(8,128)(2,1)}, u32[]{:S(2)}) %copy-start) | copy-done | bytes 4194328
  3.8 0.0 copy-start.1
  3.8 1.6 %copy-done.1 = bf16[4,256,1024]{2,1,0:T(8,128)(2,1)S(1)} copy-done((bf16[4,256,1024]{2,1,0:T(8,128)(2,1)S(1)}, bf16[4,256,1024]{2,1,0:T(8,128)(2,1)}, u32[]{:S(2)}) %copy-start.1) | copy-done | bytes 2097176
  5.4 0.0 copy-start.2
  5.4 1.0 %copy-done.2 = bf16[256,1024]{1,0:T(8,128)(2,1)S(1)} copy-done((bf16[256,1024]{1,0:T(8,128)(2,1)S(1)}, bf16[256,1024]{1,0:T(8,128)(2,1)}, u32[]{:S(2)}) %copy-start.2) | copy-done | bytes 524312
  6.4 0.0 copy-start.3
  6.4 0.7 copy-done.3
  7.1 0.0 copy-start.4
  7.1 0.7 copy-done.4
  7.8 83.3 %shard_map.73 = bf16[48,1024]{1,0:T(8,128)(2,1)S(1)} custom-call(s32[32]{0:T(128)S(1)} %bitcast.1, s32[32]{0:T(128)S(1)} %copy-done.4, bf16[1,1024]{1,0:T(2,128)(2,1)S(1)} %reshape.9.gain, bf16[48,1024]{1,0:T(8,128)(2,1)S(1)} %reshape.10.dec, bf16[4,256,1024]{2,1,0:T(8,128)(2,1)S(1)} %copy-done.1, bf16[1024,2048]{1,0:T(8,128)(2,1)S(1)} %copy-done, ...), custom_call_target="tpu_custom_call" | custom-call | tf_op jit(solution)/shard_map/pallas_call | solution.py:568
  91.1 0.7 reshape.11
Async XLA Ops:
  1.6 2.2 %copy-start = (bf16[1024,2048]{1,0:T(8,128)(2,1)S(1)}, bf16[1024,2048]{1,0:T(8,128)(2,1)}, u32[]{:S(2)}) copy-start(bf16[1024,2048]{1,0:T(8,128)(2,1)} %wkv.1) | copy-start | bytes 12582916
  3.8 1.6 %copy-start.1 = (bf16[4,256,1024]{2,1,0:T(8,128)(2,1)S(1)}, bf16[4,256,1024]{2,1,0:T(8,128)(2,1)}, u32[]{:S(2)}) copy-start(bf16[4,256,1024]{2,1,0:T(8,128)(2,1)} %tok.1) | copy-start | bytes 6291460
  5.4 1.0 %copy-start.2 = (bf16[256,1024]{1,0:T(8,128)(2,1)S(1)}, bf16[256,1024]{1,0:T(8,128)(2,1)}, u32[]{:S(2)}) copy-start(bf16[256,1024]{1,0:T(8,128)(2,1)} %wq.1) | copy-start | bytes 1572868
  6.4 0.7 copy-start.3
  7.1 0.7 copy-start.4

commit v2 on v1

v2 whole, which is shorter than its diff:
```python
import jax
import jax.numpy as jnp
from jax import lax
from jax.experimental import pallas as pl
from jax.experimental.pallas import tpu as pltpu
from jax.sharding import PartitionSpec as P

MESH = pl.DeviceIdType.MESH
F32 = jnp.float32
BF16 = jnp.bfloat16
HD = 128
NT = 8
ROWS = 48
HALF = 128
EPS = 1e-05
N_SEND = 260
N_RECV = 180


def kernel(
    assign,
    lens,
    gain,
    dec,
    tok,
    wkv,
    wq,
    out,
    wkv_v,
    tokv,
    tokx,
    xp,
    x2,
    pbuf,
    xag,
    xn,
    xin,
    wq_v,
    ssp,
    gains,
    dks,
    dkr,
    qs,
    qr,
    send_l,
    recv_l,
    send_s,
    recv_s,
    kv,
    lsem,
    ssem,
    rsem,
):
    s, g, t = lax.axis_index("sect"), lax.axis_index("grp"), lax.axis_index("tp")
    core = lax.rem(g, 2)
    sib = g + 1 - 2 * core
    xr, xl, xo = lax.rem(g + 2, 8), lax.rem(g + 6, 8), lax.rem(g + 4, 8)

    def zed(k):
        return lax.rem(t + (k + 2 * NT), NT)

    def sec(k):
        return lax.rem(s + k, 4)

    counts = {"s": 0, "r": 0}

    def new(kind, number=1):
        first = counts[kind]
        counts[kind] += number
        return first

    pending = []

    def remote(src, dst, snd, rcv, dev):
        return pltpu.make_async_remote_copy(
            src_ref=src,
            dst_ref=dst,
            send_sem=ssem.at[snd],
            recv_sem=rsem.at[rcv],
            device_id=dev,
            device_id_type=MESH,
        )

    def push(src, dst, rcv, dev, like, guard=None):
        snd = new("s")
        remote(src, dst, snd, rcv, dev).start()
        pending.append((guard, like, snd))

    def arrive(dst, rcv):
        remote(dst, dst, 0, rcv, (s, sib, t)).wait_recv()

    when = pl.when
    decoding, root = s > 0, s == 0
    first, third = s == 1, s == 3
    side, middle = first | third, s == 2

    def tok_half():
        return tokv.at[0, 0:HALF]

    def w_block():
        return wq_v.at[0:256]

    def w_half():
        return wq_v.at[0:128]

    def kv_half():
        return kv.at[0, 0:HALF]

    def kv_whole():
        return kv.at[0]

    def x_chunk():
        return xag.at[0]

    barrier = pltpu.get_barrier_semaphore()
    friends = [(s, g, zed(k)) for k in range(1, NT)]
    friends += [(sec(k), g, t) for k in (1, 2, 3)]
    friends += [(s, xr, t), (s, xl, t), (s, sib, t)]
    for dev in friends:
        pl.semaphore_signal(barrier, inc=1, device_id=dev, device_id_type=MESH)

    def load_tok(i):
        return pltpu.make_async_copy(tok.at[2 * i], tokv.at[i], lsem.at[2 + i])

    def load_out(i):
        return pltpu.make_async_copy(tok.at[2 * i + 1], tokx.at[i], lsem.at[12 + i])

    load_wq = pltpu.make_async_copy(wq, wq_v.at[pl.ds(g * 256, 256)], lsem.at[1])

    def load_wkv(a):
        return pltpu.make_async_copy(
            wkv.at[:, a * 256 : (a + 1) * 256], wkv_v.at[a], lsem.at[4 + a]
        )

    load_wq.start()

    @when(root)
    def _():
        load_tok(0).start()
        load_out(0).start()
        load_out(1).start()

    for a in range(NT):
        load_wkv(a).start()

    @when(root)
    def _():
        load_tok(1).start()

    gain_v = gain[...].astype(F32)
    gain_f = jnp.concatenate([gain_v[n : n + 1] for n in range(8)], axis=1)
    ones = jnp.ones((8, 1024), BF16)
    nt_dims = (((1,), (1,)), ((), ()))

    def column(row):
        return jnp.broadcast_to(row, (128, 128)).T

    gains[t] = gain_v

    @when(decoding)
    def _():
        xag[t] = dec[...]

    def way_of(i):
        return -1 if i == 0 else 1

    def parts(i, first, last, rows=slice(0, 256)):
        def one(n, carry):
            odd = lax.rem(n, 2)
            shift = way_of(i) * (1 - 2 * odd) * (4 - n // 2 - odd)
            head = lax.rem(t + shift + 2 * NT, NT)
            pbuf[i, n, rows] = jnp.dot(xp[i, rows], wkv_v[head], preferred_element_type=F32)
            return carry

        lax.fori_loop(first, last, one, 0)

    def prepare(i, low=0, high=8):
        def one(n, carry):
            rows = pl.ds(pl.multiple_of(n * 32, 32), 32)
            values = tokv[i, rows].astype(F32)
            xp[i, rows] = (values * gain_f).astype(BF16)
            x2[rows] = (values * values).astype(BF16)
            return carry

        lax.fori_loop(low, high, one, 0)

    @when(root)
    def _():
        load_tok(0).wait()
        for a in range(NT):
            load_wkv(a).wait()
        prepare(0)
        parts(0, 0, 2)

    pl.semaphore_wait(barrier, len(friends))

    r_long = new("r", 16)
    r_short = new("r", 12)
    r_ssp = new("r", 16)
    r_gain = new("r", 8)
    r_tok = new("r", 2)
    r_w = new("r", 4)
    r_ws = new("r", 4)
    r_xag = new("r", 8)
    r_dkv = new("r", 8)
    r_xin = new("r", 6)

    @when(root)
    def _():
        for i in range(2):
            load_out(i).wait()
        for u in range(2):
            rows = pl.ds(u * HALF, HALF)
            push(tokx.at[0, rows], tokv.at[0, rows], r_tok + u, (1, g, t), tok_half, root)
            push(tokx.at[1, rows], tokv.at[0, rows], r_tok + u, (3, g, t), tok_half, root)

    mine = pl.ds(g * 256, 256)
    load_wq.wait()
    push(wq_v.at[mine], wq_v.at[mine], r_w, (s, xr, t), w_block)
    push(wq_v.at[mine], wq_v.at[mine], r_w + 1, (s, xl, t), w_block)
    push(wq_v.at[mine], wq_v.at[mine], r_ws, (s, sib, t), w_block)

    def start_x():
        push(xag.at[t], xag.at[t], r_xag, (s, g, zed(1)), x_chunk, decoding)
        push(xag.at[t], xag.at[t], r_xag + 4, (s, g, zed(-1)), x_chunk, decoding)
        for k in range(1, NT):
            push(
                gains.at[t], gains.at[t], r_gain + k, (s, g, zed(k)), lambda: gains.at[0], decoding
            )

    def gather_x(k):
        low, high = zed(-k), zed(k)
        arrive(xag.at[low], r_xag + k - 1)
        if k < 4:
            push(xag.at[low], xag.at[low], r_xag + k, (s, g, zed(1)), x_chunk, decoding)
            arrive(xag.at[high], r_xag + 4 + k - 1)
            if k < 3:
                push(xag.at[high], xag.at[high], r_xag + 4 + k, (s, g, zed(-1)), x_chunk, decoding)

    def normalise():
        for k in range(1, NT):
            arrive(gains.at[zed(-k)], r_gain + k)

        def add(q, total):
            for n in range(8):
                x = xag[q, :, n * 128 : (n + 1) * 128].astype(F32)
                total = total + x * x
            return total

        total = lax.fori_loop(0, NT, add, jnp.zeros((ROWS, 128), F32))
        mean = jnp.sum(total, axis=1, keepdims=True) / (NT * 1024)
        scale = jnp.broadcast_to(lax.rsqrt(mean + EPS), (ROWS, 128))

        def one(q, carry):
            for n in range(8):
                cols = slice(n * 128, (n + 1) * 128)
                x = xag[q, :, cols].astype(F32) * scale * gains[q, n : n + 1]
                xn[q, :, cols] = x.astype(BF16)
            return carry

        lax.fori_loop(0, NT, one, 0)
        place = pl.ds((s - 1) * ROWS, ROWS)
        for dest in range(4):
            snd = new("s", 2)

            @when(s != dest)
            def _():
                for b in range(2):
                    remote(
                        xn.at[2 * dest + b],
                        xin.at[b, place],
                        snd + b,
                        r_xin + (s - 1) * 2 + b,
                        (dest, g, t),
                    ).start()

            for b in range(2):
                pending.append((lambda dest=dest: decoding & (s != dest), x_chunk, snd + b))
        for b in range(2):
            xin[b, place] = xn[2 * s + b]

    def own_partial():
        def one(n, carry):
            a = lax.rem(t + n, NT)
            dks[a] = jnp.dot(xn[t], wkv_v[a], preferred_element_type=F32)
            return carry

        lax.fori_loop(0, NT, one, 0)

    def send_own():
        for k in range(1, NT):
            a = zed(k)
            push(dks.at[a], dkr.at[t], r_dkv + k, (s, g, a), lambda: dks.at[0], decoding)

    def forward_w(guard):
        left, right = pl.ds(xl * 256, 128), pl.ds(xr * 256 + 128, 128)
        arrive(wq_v.at[pl.ds(xl * 256, 256)], r_w)
        push(wq_v.at[left], wq_v.at[left], r_w + 2, (s, xr, t), w_half, guard)
        arrive(wq_v.at[pl.ds(xr * 256, 256)], r_w + 1)
        push(wq_v.at[right], wq_v.at[right], r_w + 3, (s, xl, t), w_half, guard)
        for n, other in ((1, xl), (2, xr)):
            whole = pl.ds(other * 256, 256)
            push(wq_v.at[whole], wq_v.at[whole], r_ws + n, (s, sib, t), w_block, guard)

    def finish_w(guard):
        arrive(wq_v.at[pl.ds(xo * 256, 128)], r_w + 2)
        arrive(wq_v.at[pl.ds(xo * 256 + 128, 128)], r_w + 3)
        whole = pl.ds(xo * 256, 256)
        push(wq_v.at[whole], wq_v.at[whole], r_ws + 3, (s, sib, t), w_block, guard)
        for n, other in enumerate((g, xl, xr, xo)):
            block = other + 1 - 2 * core
            arrive(wq_v.at[pl.ds(block * 256, 256)], r_ws + n)

    def squares(i, guard):
        ssp[i, t] = lax.dot_general(ones, x2[...], nt_dims, preferred_element_type=F32)
        for k in range(1, NT):
            push(
                ssp.at[i, t],
                ssp.at[i, t],
                r_ssp + 8 * i + k,
                (s, g, zed(k)),
                lambda: ssp.at[0, 0],
                guard,
            )

    def ring(i, k, guard, halves=(0, 1)):
        way = way_of(i)
        for u in halves:
            rows = slice(u * HALF, (u + 1) * HALF)
            for short in (0, 1):
                if short and k == 3:
                    continue
                snd, rcv, base, steps, dev = (
                    (send_s, recv_s, r_short, 3, (s, g, zed(-way)))
                    if short
                    else (send_l, recv_l, r_long, 4, (s, g, zed(way)))
                )
                value = pbuf[i, 2 * k + short, rows]
                if k > 0:
                    arrive(rcv.at[i, k - 1, rows], base + (i * steps + k - 1) * 2 + u)
                    value = value + rcv[i, k - 1, rows].astype(F32)
                snd[i, k, rows] = value.astype(BF16)
                push(
                    snd.at[i, k, rows],
                    rcv.at[i, k, rows],
                    base + (i * steps + k) * 2 + u,
                    dev,
                    kv_half,
                    guard,
                )

    def begin(i, guard):
        prepare(i)
        parts(i, 0, 2)
        ring(i, 0, guard)
        parts(i, 2, 8)
        squares(i, guard)

    def settle(i, slot):
        for k in range(1, NT):
            arrive(ssp.at[i, zed(-k)], r_ssp + 8 * i + k)
        total = ssp[i, 0]
        for n in range(1, NT):
            total = total + ssp[i, n]
        scale = lax.rsqrt(total[0:1] / (NT * 1024) + EPS)
        for u in range(2):
            rows = slice(u * HALF, (u + 1) * HALF)
            by = column(scale[:, rows])
            arrive(recv_l.at[i, 3, rows], r_long + (i * 4 + 3) * 2 + u)
            arrive(recv_s.at[i, 2, rows], r_short + (i * 3 + 2) * 2 + u)
            value = pbuf[i, 7, rows] + recv_l[i, 3, rows].astype(F32)
            value = value + recv_s[i, 2, rows].astype(F32)
            kv[slot, rows] = jnp.concatenate(
                [value[:, :128] * by, value[:, 128:] * by], axis=1
            ).astype(BF16)

    r_y = new("r", 4)

    def here(j):
        return 4 * g + j

    def send_y(j, sections, guard):
        for dest in sections:
            push(kv.at[here(j)], kv.at[here(j)], r_y + j, (dest, g, t), kv_whole, guard)

    r_q = new("r", 4)

    def queries(guard):
        finish_w(guard)

        for other in (1, 2, 3):

            @when(s != other)
            def _():
                for b in range(2):
                    arrive(
                        xin.at[b, (other - 1) * ROWS : other * ROWS], r_xin + (other - 1) * 2 + b
                    )

        def one(n, carry):
            cols = pl.ds(pl.multiple_of(n * 256, 256), 256)
            value = jnp.dot(xin[0], wq_v[0:1024, cols], preferred_element_type=F32)
            value = value + jnp.dot(xin[1], wq_v[1024:2048, cols], preferred_element_type=F32)
            for dest in range(3):
                qs[dest, :, cols] = value[dest * ROWS : (dest + 1) * ROWS].astype(BF16)
            return carry

        lax.fori_loop(0, 4, one, 0)

    def answer(guard):
        for dest in (1, 2, 3):
            snd = new("s")

            @when(s != dest)
            def _():
                remote(qs.at[dest - 1], qr.at[s], snd, r_q + s, (dest, g, t)).start()

            pending.append((lambda dest=dest: guard & (s != dest), lambda: qs.at[0], snd))

    @when(decoding)
    def _():
        start_x()
        for a in range(NT):
            load_wkv(a).wait()

    r_x = new("r", 24)
    r_c = new("r", 16)

    near = 1 + 2 * (s // 3)
    far = 4 - near

    def entry(j):
        if isinstance(j, int):
            arrive(kv.at[here(j)], r_y + j)
        else:

            @when(s != j)
            def _():
                arrive(kv.at[here(j)], r_y + j)

        block = kv.at[here(j)]
        top, bottom = kv.at[here(j), 0:HALF], kv.at[here(j), HALF : 2 * HALF]
        push(top, top, r_x + 6 * j, (s, xr, t), kv_half, decoding)
        push(bottom, bottom, r_x + 6 * j + 1, (s, xl, t), kv_half, decoding)
        push(bottom, bottom, r_x + 6 * j + 4, (s, xr, t), kv_half, decoding)
        push(top, top, r_x + 6 * j + 5, (s, xl, t), kv_half, decoding)
        push(block, block, r_c + 4 * j, (s, sib, t), kv_whole, decoding)

    def relay(j):
        left, right = 4 * xl + j, 4 * xr + j
        part_l = kv.at[left, 0:HALF]
        arrive(part_l, r_x + 6 * j)
        push(part_l, part_l, r_x + 6 * j + 2, (s, xr, t), kv_half, decoding)
        part_r = kv.at[right, HALF : 2 * HALF]
        arrive(part_r, r_x + 6 * j + 1)
        push(part_r, part_r, r_x + 6 * j + 3, (s, xl, t), kv_half, decoding)
        arrive(kv.at[left, HALF : 2 * HALF], r_x + 6 * j + 4)
        push(kv.at[left], kv.at[left], r_c + 4 * j + 1, (s, sib, t), kv_whole, decoding)
        arrive(kv.at[right, 0:HALF], r_x + 6 * j + 5)
        push(kv.at[right], kv.at[right], r_c + 4 * j + 2, (s, sib, t), kv_whole, decoding)

    def opposite(j):
        block = 4 * xo + j
        arrive(kv.at[block, 0:128], r_x + 6 * j + 2)
        arrive(kv.at[block, 128:256], r_x + 6 * j + 3)
        push(kv.at[block], kv.at[block], r_c + 4 * j + 3, (s, sib, t), kv_whole, decoding)

    def crossed(j):
        for n, other in enumerate((g, xl, xr, xo)):
            arrive(kv.at[4 * (other + 1 - 2 * core) + j], r_c + 4 * j + n)

    def tokens(u):
        rows = slice(u * HALF, (u + 1) * HALF)
        arrive(tokv.at[0, rows], r_tok + u)
        prepare(0, 4 * u, 4 * u + 4)
        parts(0, 0, 2, rows)
        ring(0, 0, side, (u,))
        parts(0, 2, 8, rows)

    def settle_side():
        settle(0, here(s))

        @when(s == 1)
        def _():
            send_y(1, (2, 3), first)

        @when(s == 3)
        def _():
            send_y(3, (2, 1), third)

    @when(root)
    def _():
        ring(0, 0, root)
        squares(0, root)
        parts(0, 2, 8)
        load_tok(1).wait()
        ring(0, 1, root)
        prepare(1)
        parts(1, 0, 2)
        ring(1, 0, root)
        parts(1, 2, 8)
        ring(0, 2, root)
        ring(1, 1, root)
        squares(1, root)
        ring(0, 3, root)
        ring(1, 2, root)
        forward_w(root)
        settle(0, here(0))
        send_y(0, (1, 3, 2), root)
        ring(1, 3, root)
        settle(1, here(2))
        send_y(2, (1, 3, 2), root)
        queries(root)
        answer(root)

    @when(decoding)
    def _():
        gather_x(1)
        gather_x(2)

        @when(side)
        def _():
            tokens(0)

        gather_x(3)

        @when(side)
        def _():
            ring(0, 1, side, (0,))
            tokens(1)
            squares(0, side)

        forward_w(decoding)
        gather_x(4)
        normalise()

        @when(side)
        def _():
            ring(0, 2, side, (0,))
            ring(0, 1, side, (1,))


        @when(side)
        def _():
            ring(0, 3, side, (0,))
            ring(0, 2, side, (1,))

        own_partial()

        @when(side)
        def _():
            ring(0, 3, side, (1,))

        @when(s == 2)
        def _():
            queries(middle)
            answer(middle)

        entry(0)

        @when(side)
        def _():
            settle_side()

        entry(near)

        @when(side)
        def _():
            queries(side)
            answer(side)

        send_own()

    inv = 1.0 / HD**0.5

    @when(root)
    def _():
        out[...] = jnp.zeros(out.shape, out.dtype)

    @when(decoding)
    def _():
        relay(0)
        entry(2)
        entry(far)
        relay(near)
        opposite(0)
        relay(2)
        relay(far)
        opposite(near)
        opposite(2)
        opposite(far)

        for k in range(1, NT):
            arrive(dkr.at[zed(-k)], r_dkv + k)
        own = dks[t]
        for k in range(1, NT):
            own = own + dkr[zed(k)]
        own_k, own_v = own[:, :128].astype(BF16), own[:, 128:].astype(BF16)
        for src in range(4):

            @when(s != src)
            def _():
                arrive(qr.at[src], r_q + src)

            if src > 0:

                @when(s == src)
                def _():
                    qr[src] = qs[src - 1]

        group = (s - 1) * 8 + g

        def pick(p, carry):
            seen, i0, i1, i2, n0, n1, n2 = carry
            hit = (assign[p] == group).astype(jnp.int32)
            length = lens[p]
            h0 = hit * (seen == 0).astype(jnp.int32)
            h1 = hit * (seen == 1).astype(jnp.int32)
            h2 = hit * (seen == 2).astype(jnp.int32)
            return (
                seen + hit,
                i0 + h0 * p,
                i1 + h1 * p,
                i2 + h2 * p,
                n0 + h0 * length,
                n1 + h1 * length,
                n2 + h2 * length,
            )

        zero = jnp.int32(0)
        picked = lax.fori_loop(0, assign.shape[0], pick, (zero,) * 7)
        low = jnp.float32(-1e30)
        pos = lax.broadcasted_iota(jnp.int32, (128, 256), 1)
        row = lax.rem(lax.broadcasted_iota(jnp.int32, (128, 16), 0), 16)
        col = lax.broadcasted_iota(jnp.int32, (128, 16), 1)
        mask_own = (row // 2 == col // 2) & (col <= row)
        asked, selves = [], []
        for j in range(3):
            rows = slice(j * 16, (j + 1) * 16)
            raw = qr[0, rows].astype(F32)
            for src in range(1, 4):
                raw = raw + qr[src, rows].astype(F32)
            q = jnp.concatenate(
                [raw[:, h * 128 : (h + 1) * 128] for h in range(8)], axis=0
            ).astype(BF16)
            asked.append(q)
            selves.append(
                lax.dot_general(q, own_k[rows], nt_dims, preferred_element_type=F32) * inv
            )
        for j in range(4):
            crossed(j)
        for j in range(3):
            rows = slice(j * 16, (j + 1) * 16)
            block = kv[picked[1 + j]]
            keys, values = block[:, :128], block[:, 128:]
            q, self_ = asked[j], selves[j]
            pre = lax.dot_general(q, keys, nt_dims, preferred_element_type=F32) * inv
            mask_pre = pos < picked[4 + j]
            pre = jnp.where(mask_pre, pre, low)
            self_ = jnp.where(mask_own, self_, low)
            top = jnp.maximum(
                jnp.max(pre, axis=1, keepdims=True), jnp.max(self_, axis=1, keepdims=True)
            )
            e_pre = jnp.where(mask_pre, jnp.exp(pre - top), 0.0)
            e_own = jnp.where(mask_own, jnp.exp(self_ - top), 0.0)
            norm = jnp.sum(e_pre, axis=1, keepdims=True) + jnp.sum(e_own, axis=1, keepdims=True)
            w_pre = (e_pre / norm).astype(BF16)
            w_own = (e_own / norm).astype(BF16)
            o = jnp.dot(w_pre, values, preferred_element_type=F32)
            o = o + jnp.dot(w_own, own_v[rows], preferred_element_type=F32)
            o = o.astype(BF16)
            for h in range(8):
                out[rows, h * 128 : (h + 1) * 128] = o[h * 16 : (h + 1) * 16]

    for guard, like, snd in pending:

        def done(like=like, snd=snd):
            remote(like(), like(), snd, 0, (s, sib, t)).wait_send()

        if guard is None:
            done()
        else:
            when(guard() if callable(guard) else guard)(done)

    assert counts["s"] <= N_SEND and counts["r"] <= N_RECV, counts


def local(
    prefix_tokens, prefix_lengths, assignment, norm_gain, kv_weight, query_weight, decode_tokens
):
    shape = decode_tokens.shape
    smem = pl.BlockSpec(memory_space=pltpu.SMEM)
    vmem = pl.BlockSpec(memory_space=pltpu.VMEM)
    anywhere = pl.BlockSpec(memory_space=pl.ANY)
    result = pl.pallas_call(
        kernel,
        out_shape=jax.ShapeDtypeStruct((ROWS, 1024), BF16),
        in_specs=[smem, smem, vmem, vmem, anywhere, anywhere, anywhere],
        out_specs=vmem,
        scratch_shapes=[
            pltpu.VMEM((8, 1024, 256), BF16),
            pltpu.VMEM((2, 256, 1024), BF16),
            pltpu.VMEM((2, 256, 1024), BF16),
            pltpu.VMEM((2, 256, 1024), BF16),
            pltpu.VMEM((256, 1024), BF16),
            pltpu.VMEM((2, 8, 256, 256), F32),
            pltpu.VMEM((8, ROWS, 1024), BF16),
            pltpu.VMEM((8, ROWS, 1024), BF16),
            pltpu.VMEM((2, 3 * ROWS, 1024), BF16),
            pltpu.VMEM((2048, 1024), BF16),
            pltpu.VMEM((2, 8, 8, 256), F32),
            pltpu.VMEM((8, 8, 128), F32),
            pltpu.VMEM((8, ROWS, 256), F32),
            pltpu.VMEM((8, ROWS, 256), F32),
            pltpu.VMEM((3, ROWS, 1024), BF16),
            pltpu.VMEM((4, ROWS, 1024), BF16),
            pltpu.VMEM((2, 4, 256, 256), BF16),
            pltpu.VMEM((2, 4, 256, 256), BF16),
            pltpu.VMEM((2, 3, 256, 256), BF16),
            pltpu.VMEM((2, 3, 256, 256), BF16),
            pltpu.VMEM((32, 256, 256), BF16),
            pltpu.SemaphoreType.DMA((14,)),
            pltpu.SemaphoreType.DMA((N_SEND,)),
            pltpu.SemaphoreType.DMA((N_RECV,)),
        ],
        compiler_params=pltpu.CompilerParams(
            collective_id=0, has_side_effects=True, vmem_limit_bytes=60 * 2**20
        ),
    )(
        assignment[:, 0],
        prefix_lengths,
        norm_gain.reshape(8, 128),
        decode_tokens.reshape(ROWS, 1024),
        prefix_tokens,
        kv_weight,
        query_weight,
    )
    return result.reshape(shape)


def solution(mesh):
    placed = (
        P(("sect", "grp"), None, "tp"),
        P(),
        P(),
        P("tp"),
        P("tp", None),
        P(("sect", "grp"), "tp"),
        P(("sect", "grp"), None, None, None, "tp"),
    )
    return jax.shard_map(
        local,
        mesh=mesh,
        in_specs=placed,
        out_specs=P(("sect", "grp"), None, None, None, "tp"),
        check_vma=False,
    )
```

time: 92 us -> 67.6 us (0.73)
  Pallas kernels: 83.3 us -> 63.8 us
  local copies, waits for them, and re-layouts: 8.42 us -> 3.14 us
    pallas_call x1, Pallas kernels: 83.3 us -> 63.8 us  [local(): pl.pallas_call(kernel, out_shape=jax.ShapeDtypeStruct((ROWS, 1024), BF16)...]
    unnamed x10 -> x0, local copies, waits for them, and re-layouts: 6.12 us -> none
where the time goes in v2:
time: 67.6 us; the launch traced here: 66.9 us
  Pallas kernels  63.8 us (94%)
  local copies, waits for them, and re-layouts  3.14 us (5%)
    pallas_call x1, Pallas kernels, local(): pl.pallas_call(kernel, out_shape=jax.ShapeDtypeStruct((ROWS, 1024), BF16)...  63.8 us
    reshape x1, local copies, waits for them, and re-layouts, local(): return result.reshape(shape)  1.57 us
    reshape x1, local copies, waits for them, and re-layouts, local(): decode_tokens.reshape(ROWS, 1024)  1.57 us

profile of v2, /device:TPU:17, one launch (start us, length us, event | category | flops | bytes accessed | tf_op | source)
XLA Modules:
  0.0 66.9 jit_solution(15919468259308204204)
XLA Ops:
  0.0 1.6 %reshape.10.dec = bf16[48,1024]{1,0:T(8,128)(2,1)} reshape(bf16[1,3,8,2,1024]{4,3,2,1,0:T(2,128)(2,1)} %param.13) | data formatting | bytes 196608 | tf_op jit(solution)/shard_map/reshape | solution.py:733
  1.6 63.8 %shard_map.73 = bf16[48,1024]{1,0:T(8,128)(2,1)} custom-call(s32[32]{0:T(128)} %bitcast.3, s32[32]{0:T(128)} %lens.1, bf16[8,128]{1,0:T(8,128)(2,1)} %bitcast.2, bf16[48,1024]{1,0:T(8,128)(2,1)} %reshape.10.dec, bf16[4,256,1024]{2,1,0:T(8,128)(2,1)} %tok.1, bf16[1024,2048]{1,0:T(8,128)(2,1)} %wkv.1, bf16[256,1024]{1,0:T(8,128)(2,1)} %wq.1), custom_call_target="tpu_custom_call" | custom-call | tf_op jit(solution)/shard_map/pallas_call | solution.py:695
  65.4 1.6 %reshape.11 = bf16[1,3,8,2,1024]{4,3,2,1,0:T(2,128)(2,1)} reshape(bf16[48,1024]{1,0:T(8,128)(2,1)} %shard_map.73) | data formatting | bytes 196608 | tf_op jit(solution)/shard_map/reshape | solution.py:738
